TPU v7x, 32 devices: a whole 2x2x4 slice. The times are simulated.
32 devices in a mesh: section: 4 (over z), tm: 4 (over y, x), batch: 2 (over core).
Axes of the slice: x: 2, y: 2, z: 4, core: 2. Of those that a mesh axis runs over, the one named last changes fastest.
Arguments:
- acts: bfloat16 [4, 4, 8, 6, 10240], P('section', 'batch', 'tm'), may hold values from -6 to 6
- cot: bfloat16 [4, 8, 6, 10240], P('batch', 'tm'), may hold values from -6 to 6
- spatial_weight: bfloat16 [4, 9, 64, 64], P('section'), may hold values from -0.25 to 0.25
- temporal_weight: bfloat16 [4, 3, 64, 64], P('section'), may hold values from -0.4375 to 0.4375
Outputs:
- grad_in: bfloat16 [4, 4, 8, 6, 10240], P('section', 'batch', 'tm')
- grad_spatial: float32 [4, 9, 64, 64], P('section')
- grad_temporal: float32 [4, 3, 64, 64], P('section')
All inputs are finite; a program needn't handle non-finite values.
Results may differ from a plain program's by a relative error of at most 0.012.
Values may be sent and summed in bfloat16 or wider, within the bound.
A program may use at most 128 MiB of HBM per device.

v0:
```python
import jax
import jax.numpy as jnp
from jax import lax
from jax.sharding import PartitionSpec as P

TIME_DILATION = 2


def from_behind(value, axis, steps):
    count = lax.axis_size(axis)
    first, last = (max(0, -steps), min(count, count - steps))
    return lax.ppermute(value, axis, [(source, source + steps) for source in range(first, last)])


def split_pixels(a, chans):
    return a.reshape(a.shape[:-1] + (a.shape[-1] // chans, chans))


def paired_kernel(kernel):
    return jnp.kron(jnp.eye(2, dtype=kernel.dtype), kernel)


def spatial_fwd(x, ws):
    rows, width = (x.shape[1], x.shape[2])
    chans = ws.shape[-1]
    padded = jnp.pad(x, ((0, 0), (1, 1), (chans, chans)))
    total = jnp.zeros(x.shape, jnp.float32)
    for i in range(3):
        for j in range(3):
            piece = split_pixels(padded[:, i : i + rows, j * chans : j * chans + width], 2 * chans)
            total = total + jnp.einsum(
                "nrpa,ab->nrpb",
                piece,
                paired_kernel(ws[3 * i + j]),
                preferred_element_type=jnp.float32,
            ).reshape(x.shape)
    return total


def spatial_back(gz, x, ws):
    rows, width = (x.shape[1], x.shape[2])
    chans = ws.shape[-1]
    xpad = jnp.pad(x, ((0, 0), (1, 1), (chans, chans)))
    gradient_padded = jnp.pad(gz, ((0, 0), (1, 1), (chans, chans)))
    gz_pairs = split_pixels(gz, 2 * chans)
    total = jnp.zeros(x.shape, jnp.float32)
    grads = []
    for i in range(3):
        for j in range(3):
            gpiece = split_pixels(
                gradient_padded[:, 2 - i : 2 - i + rows, (2 - j) * chans : (2 - j) * chans + width],
                2 * chans,
            )
            total = total + jnp.einsum(
                "nrpb,ab->nrpa",
                gpiece,
                paired_kernel(ws[3 * i + j]),
                preferred_element_type=jnp.float32,
            ).reshape(x.shape)
            xpiece = split_pixels(xpad[:, i : i + rows, j * chans : j * chans + width], 2 * chans)
            square = jnp.einsum(
                "nrpa,nrpb->ab", xpiece, gz_pairs, preferred_element_type=jnp.float32
            )
            grads.append(square[:chans, :chans] + square[chans:, chans:])
    return (total, jnp.stack(grads))


def temporal_back(h, gradient_piece, gradient_padded, dilation_step, wt):
    count = gradient_piece.shape[0]
    chans = wt.shape[-1]
    kernel_taps = [
        gradient_padded[2 * dilation_step : 2 * dilation_step + count],
        gradient_piece,
        gradient_padded[0:count],
    ]
    h_pix = split_pixels(h, chans)
    gh = jnp.zeros(gradient_piece.shape, jnp.float32)
    tgrads = []
    for k in range(3):
        tap = split_pixels(kernel_taps[k], chans)
        gh = gh + jnp.einsum(
            "trwd,cd->trwc", tap, wt[k], preferred_element_type=jnp.float32
        ).reshape(gradient_piece.shape)
        tgrads.append(jnp.einsum("trwc,trwd->cd", h_pix, tap, preferred_element_type=jnp.float32))
    return (gh.astype(jnp.bfloat16), jnp.stack(tgrads))


def section_backward(x, gradient_piece, ws, wt):
    dilation_step = TIME_DILATION
    z = spatial_fwd(x, ws)
    sig = jax.nn.sigmoid(z)
    h = (z * sig).astype(jnp.bfloat16)
    deriv = sig * (1.0 + z * (1.0 - sig))
    tile_gradient, h_tile = (
        lax.all_to_all(gradient_piece, "tm", split_axis=2, concat_axis=0, tiled=True),
        lax.all_to_all(h, "tm", split_axis=2, concat_axis=0, tiled=True),
    )
    gradient_padded = jnp.pad(tile_gradient, ((dilation_step, dilation_step), (0, 0), (0, 0)))
    gh_tile, tgrads = temporal_back(h_tile, tile_gradient, gradient_padded, dilation_step, wt)
    gh = lax.all_to_all(gh_tile, "tm", split_axis=0, concat_axis=2, tiled=True)
    gz = (gh.astype(jnp.float32) * deriv).astype(jnp.bfloat16)
    back, sgrads = spatial_back(gz, x, ws)
    result = (gradient_piece.astype(jnp.float32) + back).astype(jnp.bfloat16)
    return (result, sgrads, tgrads)


def body(acts, cot, spatial_weight, temporal_weight):
    section_idx = lax.axis_index("section")
    number_sections = lax.axis_size("section")
    micro = acts.shape[1]
    local_acts = acts[0]
    ws = spatial_weight[0]
    wt = temporal_weight[0]
    received = jnp.zeros(cot.shape[1:], jnp.bfloat16)
    grads_in = jnp.zeros(local_acts.shape, jnp.bfloat16)
    acc_spatial = jnp.zeros(ws.shape, jnp.float32)
    acc_temporal = jnp.zeros(wt.shape, jnp.float32)
    total_turns = micro + number_sections - 1
    for turn in range(total_turns):
        which = jnp.int32(turn) - (number_sections - 1 - section_idx)
        valid = jnp.logical_and(which >= 0, which < micro)
        clipped = jnp.clip(which, 0, micro - 1)
        x_now = lax.dynamic_index_in_dim(local_acts, clipped, 0, keepdims=False)
        top_grad = lax.dynamic_index_in_dim(cot, clipped, 0, keepdims=False)
        incoming = jnp.where(section_idx == number_sections - 1, top_grad, received)
        result, sgrads, tgrads = section_backward(x_now, incoming, ws, wt)
        weight = valid.astype(jnp.float32)
        acc_spatial = acc_spatial + weight * sgrads
        acc_temporal = acc_temporal + weight * tgrads
        select = (jnp.arange(micro, dtype=jnp.int32) == which)[:, None, None, None]
        grads_in = jnp.where(select, result[None], grads_in)
        if turn + 1 < total_turns:
            received = from_behind(result, "section", -1)
    sum_spatial, sum_temporal = lax.psum((acc_spatial, acc_temporal), ("tm", "batch"))
    return (grads_in[None], sum_spatial[None], sum_temporal[None])


def solution(mesh):
    in_specs = (
        P("section", "batch", "tm", None, None),
        P("batch", "tm", None, None),
        P("section", None, None, None),
        P("section", None, None, None),
    )
    out_specs = (
        P("section", "batch", "tm", None, None),
        P("section", None, None, None),
        P("section", None, None, None),
    )
    return jax.shard_map(body, mesh=mesh, in_specs=in_specs, out_specs=out_specs, check_vma=False)
```

profile of v0, /device:TPU:24, one launch (start us, length us, event | category | flops | bytes accessed | tf_op | source)
XLA Modules:
  0.0 929.5 jit_solution(14927379624928204376)
XLA Ops:
  8.3 8.2 copy.623
  16.6 10.0 %reshape.1685 = bf16[4,2,15360]{2,1,0:T(2,128)(2,1)} reshape(bf16[10240,2,6]{2,1,0:T(2,128)(2,1)} %bitcast.1159) | data formatting | bytes 491520
  26.5 4.2 all-to-all-start
  75.6 3.3 pad_slice_fusion.50
  90.9 3.1 pad_slice_fusion.18
  126.4 13.6 %reshape.1686 = bf16[10240,2,6]{2,1,0:T(2,128)(2,1)} reshape(bf16[4,2,15360]{2,1,0:T(2,128)(2,1)} %all-to-all-done) | data formatting | bytes 491520
  140.0 10.6 %copy.624 = bf16[2,6,4,2560]{3,0,2,1:T(2,128)(2,1)S(1)} copy(bf16[2,6,4,2560]{1,0,3,2:T(2,128)(2,1)} %bitcast.1160) | data formatting | bytes 491520 | tf_op jit(solution)/shard_map/all_to_all | solution.py:95
  153.7 4.3 all-to-all-start.1
  159.1 4.6 all-to-all-done.1
  205.2 10.3 %copy.809 = bf16[2,6,10240]{1,0,2:T(2,128)(2,1)} copy(bf16[2,6,10240]{2,0,1:T(2,128)(2,1)} %get-tuple-element.11) | data formatting | bytes 491520 | tf_op jit(solution)/shard_map/convert_element_type | solution.py:92
  215.5 9.9 %reshape.1695 = bf16[4,2,15360]{2,1,0:T(2,128)(2,1)} reshape(bf16[10240,2,6]{2,1,0:T(2,128)(2,1)} %bitcast.1161) | data formatting | bytes 491520
  225.4 3.4 all-to-all-start.10
  233.9 8.2 copy.651
  242.1 9.9 %reshape.1687 = bf16[4,2,15360]{2,1,0:T(2,128)(2,1)} reshape(bf16[10240,2,6]{2,1,0:T(2,128)(2,1)} %bitcast.1175) | data formatting | bytes 491520
  252.0 4.2 all-to-all-start.2
  257.1 12.6 %reshape.1696 = bf16[10240,2,6]{2,1,0:T(2,128)(2,1)} reshape(bf16[4,2,15360]{2,1,0:T(2,128)(2,1)S(1)} %all-to-all-done.10) | data formatting | bytes 491520
  269.7 12.2 %copy.902 = bf16[2,6,4,2560]{3,2,0,1:T(4,128)(2,1)S(1)} copy(bf16[2,6,4,2560]{1,0,3,2:T(2,128)(2,1)} %bitcast.1162) | data formatting | bytes 491520 | tf_op jit(solution)/shard_map/all_to_all | solution.py:96
  283.3 12.6 %reshape.1688 = bf16[10240,2,6]{2,1,0:T(2,128)(2,1)} reshape(bf16[4,2,15360]{2,1,0:T(2,128)(2,1)S(1)} %all-to-all-done.2) | data formatting | bytes 491520
  296.0 10.2 %copy.652 = bf16[2,6,4,2560]{3,0,2,1:T(2,128)(2,1)S(1)} copy(bf16[2,6,4,2560]{1,0,3,2:T(2,128)(2,1)} %bitcast.1163) | data formatting | bytes 491520 | tf_op jit(solution)/shard_map/all_to_all | solution.py:95
  314.8 4.4 all-to-all-start.3
  321.1 3.8 all-to-all-done.3
  366.4 10.3 %copy.812 = bf16[2,6,10240]{1,0,2:T(2,128)(2,1)} copy(bf16[2,6,10240]{2,0,1:T(2,128)(2,1)} %get-tuple-element.9) | data formatting | bytes 491520 | tf_op jit(solution)/shard_map/convert_element_type | solution.py:92
  376.7 9.9 %reshape.1697 = bf16[4,2,15360]{2,1,0:T(2,128)(2,1)} reshape(bf16[10240,2,6]{2,1,0:T(2,128)(2,1)} %bitcast.1164) | data formatting | bytes 491520
  386.6 3.8 all-to-all-start.11
  395.5 8.1 copy.679
  403.7 9.9 %reshape.1689 = bf16[4,2,15360]{2,1,0:T(2,128)(2,1)} reshape(bf16[10240,2,6]{2,1,0:T(2,128)(2,1)} %bitcast.1176) | data formatting | bytes 491520
  413.6 4.2 all-to-all-start.4
  418.4 12.6 %reshape.1698 = bf16[10240,2,6]{2,1,0:T(2,128)(2,1)} reshape(bf16[4,2,15360]{2,1,0:T(2,128)(2,1)S(1)} %all-to-all-done.11) | data formatting | bytes 491520
  431.1 12.2 %copy.903 = bf16[2,6,4,2560]{3,2,0,1:T(4,128)(2,1)S(1)} copy(bf16[2,6,4,2560]{1,0,3,2:T(2,128)(2,1)} %bitcast.1165) | data formatting | bytes 491520 | tf_op jit(solution)/shard_map/all_to_all | solution.py:96
  444.7 12.6 %reshape.1690 = bf16[10240,2,6]{2,1,0:T(2,128)(2,1)} reshape(bf16[4,2,15360]{2,1,0:T(2,128)(2,1)S(1)} %all-to-all-done.4) | data formatting | bytes 491520
  457.3 10.2 %copy.680 = bf16[2,6,4,2560]{3,0,2,1:T(2,128)(2,1)S(1)} copy(bf16[2,6,4,2560]{1,0,3,2:T(2,128)(2,1)} %bitcast.1166) | data formatting | bytes 491520 | tf_op jit(solution)/shard_map/all_to_all | solution.py:95
  476.2 4.4 all-to-all-start.5
  482.3 3.8 all-to-all-done.5
  525.7 10.2 %copy.815 = bf16[2,6,10240]{1,0,2:T(2,128)(2,1)} copy(bf16[2,6,10240]{2,0,1:T(2,128)(2,1)} %get-tuple-element.7) | data formatting | bytes 491520 | tf_op jit(solution)/shard_map/convert_element_type | solution.py:92
  536.0 9.9 %reshape.1699 = bf16[4,2,15360]{2,1,0:T(2,128)(2,1)} reshape(bf16[10240,2,6]{2,1,0:T(2,128)(2,1)} %bitcast.1167) | data formatting | bytes 491520
  545.9 3.6 all-to-all-start.12
  554.6 8.1 copy.707
  562.8 9.9 %reshape.1691 = bf16[4,2,15360]{2,1,0:T(2,128)(2,1)} reshape(bf16[10240,2,6]{2,1,0:T(2,128)(2,1)} %bitcast.1177) | data formatting | bytes 491520
  572.7 4.2 all-to-all-start.6
  577.8 12.6 %reshape.1700 = bf16[10240,2,6]{2,1,0:T(2,128)(2,1)} reshape(bf16[4,2,15360]{2,1,0:T(2,128)(2,1)S(1)} %all-to-all-done.12) | data formatting | bytes 491520
  590.4 12.2 %copy.904 = bf16[2,6,4,2560]{3,2,0,1:T(4,128)(2,1)S(1)} copy(bf16[2,6,4,2560]{1,0,3,2:T(2,128)(2,1)} %bitcast.1168) | data formatting | bytes 491520 | tf_op jit(solution)/shard_map/all_to_all | solution.py:96
  604.0 12.6 %reshape.1692 = bf16[10240,2,6]{2,1,0:T(2,128)(2,1)} reshape(bf16[4,2,15360]{2,1,0:T(2,128)(2,1)S(1)} %all-to-all-done.6) | data formatting | bytes 491520
  616.6 10.2 %copy.708 = bf16[2,6,4,2560]{3,0,2,1:T(2,128)(2,1)S(1)} copy(bf16[2,6,4,2560]{1,0,3,2:T(2,128)(2,1)} %bitcast.1169) | data formatting | bytes 491520 | tf_op jit(solution)/shard_map/all_to_all | solution.py:95
  635.5 4.6 all-to-all-start.7
  641.9 3.8 all-to-all-done.7
  687.6 10.2 %copy.818 = bf16[2,6,10240]{1,0,2:T(2,128)(2,1)} copy(bf16[2,6,10240]{2,0,1:T(2,128)(2,1)} %get-tuple-element.5) | data formatting | bytes 491520 | tf_op jit(solution)/shard_map/convert_element_type | solution.py:92
  697.8 9.9 %reshape.1701 = bf16[4,2,15360]{2,1,0:T(2,128)(2,1)} reshape(bf16[10240,2,6]{2,1,0:T(2,128)(2,1)} %bitcast.1170) | data formatting | bytes 491520
  707.7 3.6 all-to-all-start.13
  712.9 8.1 copy.735
  721.1 9.9 %reshape.1693 = bf16[4,2,15360]{2,1,0:T(2,128)(2,1)} reshape(bf16[10240,2,6]{2,1,0:T(2,128)(2,1)} %bitcast.1178) | data formatting | bytes 491520
  731.0 4.2 all-to-all-start.8
  735.9 12.6 %reshape.1702 = bf16[10240,2,6]{2,1,0:T(2,128)(2,1)} reshape(bf16[4,2,15360]{2,1,0:T(2,128)(2,1)S(1)} %all-to-all-done.13) | data formatting | bytes 491520
  748.5 12.2 %copy.905 = bf16[2,6,4,2560]{3,2,0,1:T(4,128)(2,1)S(1)} copy(bf16[2,6,4,2560]{1,0,3,2:T(2,128)(2,1)} %bitcast.1171) | data formatting | bytes 491520 | tf_op jit(solution)/shard_map/all_to_all | solution.py:96
  762.1 12.6 %reshape.1694 = bf16[10240,2,6]{2,1,0:T(2,128)(2,1)} reshape(bf16[4,2,15360]{2,1,0:T(2,128)(2,1)S(1)} %all-to-all-done.8) | data formatting | bytes 491520
  774.7 10.2 %copy.736 = bf16[2,6,4,2560]{3,0,2,1:T(2,128)(2,1)S(1)} copy(bf16[2,6,4,2560]{1,0,3,2:T(2,128)(2,1)} %bitcast.1172) | data formatting | bytes 491520 | tf_op jit(solution)/shard_map/all_to_all | solution.py:95
  788.7 4.3 all-to-all-start.9
  795.0 3.5 all-to-all-done.9
  841.1 10.3 %copy.821 = bf16[2,6,10240]{1,0,2:T(2,128)(2,1)} copy(bf16[2,6,10240]{2,0,1:T(2,128)(2,1)} %get-tuple-element.3) | data formatting | bytes 491520 | tf_op jit(solution)/shard_map/convert_element_type | solution.py:92
  851.4 9.9 %reshape.1703 = bf16[4,2,15360]{2,1,0:T(2,128)(2,1)} reshape(bf16[10240,2,6]{2,1,0:T(2,128)(2,1)} %bitcast.1173) | data formatting | bytes 491520
  861.3 3.6 all-to-all-start.14
  866.9 3.6 all-to-all-done.14
  870.4 12.6 %reshape.1704 = bf16[10240,2,6]{2,1,0:T(2,128)(2,1)} reshape(bf16[4,2,15360]{2,1,0:T(2,128)(2,1)S(1)} %all-to-all-done.14) | data formatting | bytes 491520
  883.2 12.3 %copy.906 = bf16[2,6,4,2560]{3,2,0,1:T(4,128)(2,1)S(1)} copy(bf16[2,6,4,2560]{1,0,3,2:T(2,128)(2,1)} %bitcast.1174) | data formatting | bytes 491520 | tf_op jit(solution)/shard_map/all_to_all | solution.py:96
  897.0 23.7 %psum.15 = f32[1,3,64,64]{3,2,1,0:T(8,128)} all-reduce(f32[1,3,64,64]{3,2,1,0:T(8,128)S(1)} %fusion.170), channel_id=1, replica_groups=mesh['section'=4,'tm'=4,'batch'=2] {'tm','batch'}, use_global_device_ids=true, to_apply=%region_1.2 | all-reduce | flops 12288 | bytes 98304 | tf_op jit(solution)/shard_map/psum | solution.py:134
  (796 shorter events, 366.7 us)
Async XLA Ops:
  8.3 24.1 %copy-start.132 = (bf16[1,9,64,64]{3,2,1,0:T(8,128)(2,1)S(1)}, bf16[1,9,64,64]{3,2,1,0:T(8,128)(2,1)}, u32[]{:S(2)}) copy-start(bf16[1,9,64,64]{3,2,1,0:T(8,128)(2,1)} %param.6) | copy-start | bytes 221188
  26.5 99.9 %all-to-all-start = ((bf16[4,2,15360]{2,1,0:T(2,128)(2,1)}), bf16[4,2,15360]{2,1,0:T(2,128)(2,1)}, u32[]{:S(2)}, u32[]{:S(2)}) async-start(bf16[4,2,15360]{2,1,0:T(2,128)(2,1)} %reshape.1685), calls=%async_computation | async-start | bytes 491520 | tf_op jit(solution)/shard_map/all_to_all | solution.py:95
  33.8 160.6 %copy-start.16 = (bf16[128,128,1,1]{1,0,2,3:T(8,128)(2,1)}, bf16[128,128,1,1]{1,0,2,3:T(8,128)(2,1)S(1)}, u32[]{:S(2)}) copy-start(bf16[128,128,1,1]{1,0,2,3:T(8,128)(2,1)S(1)} %reshape.1603) | copy-start | bytes 98308
  33.9 160.8 %copy-start.11 = (bf16[128,128,1,1]{1,0,2,3:T(8,128)(2,1)}, bf16[128,128,1,1]{1,0,2,3:T(8,128)(2,1)S(1)}, u32[]{:S(2)}) copy-start(bf16[128,128,1,1]{1,0,2,3:T(8,128)(2,1)S(1)} %reshape.1604) | copy-start | bytes 98308
  34.1 160.9 %copy-start.6 = (bf16[128,128,1,1]{1,0,2,3:T(8,128)(2,1)}, bf16[128,128,1,1]{1,0,2,3:T(8,128)(2,1)S(1)}, u32[]{:S(2)}) copy-start(bf16[128,128,1,1]{1,0,2,3:T(8,128)(2,1)S(1)} %reshape.1605) | copy-start | bytes 98308
  34.2 162.0 %copy-start.1 = (bf16[128,128,1,1]{1,0,2,3:T(8,128)(2,1)}, bf16[128,128,1,1]{1,0,2,3:T(8,128)(2,1)S(1)}, u32[]{:S(2)}) copy-start(bf16[128,128,1,1]{1,0,2,3:T(8,128)(2,1)S(1)} %reshape.1606) | copy-start | bytes 98308
  34.6 159.6 %copy-start.21 = (bf16[128,128,1,1]{1,0,2,3:T(8,128)(2,1)}, bf16[128,128,1,1]{1,0,2,3:T(8,128)(2,1)S(1)}, u32[]{:S(2)}) copy-start(bf16[128,128,1,1]{1,0,2,3:T(8,128)(2,1)S(1)} %reshape.1602) | copy-start | bytes 98308
  35.7 90.1 %copy-start.43 = (bf16[2,6,80,128]{3,2,0,1:T(8,128)(2,1)}, bf16[2,6,80,128]{3,2,0,1:T(8,128)(2,1)S(1)}, u32[]{:S(2)}) copy-start(bf16[2,6,80,128]{3,2,0,1:T(8,128)(2,1)S(1)} %reshape.1505) | copy-start | bytes 737284
  153.7 9.9 %all-to-all-start.1 = ((bf16[8,6,2560]{2,1,0:T(8,128)(2,1)}), bf16[8,6,2560]{2,1,0:T(8,128)(2,1)S(1)}, u32[]{:S(2)}, u32[]{:S(2)}) async-start(bf16[8,6,2560]{2,1,0:T(8,128)(2,1)} %reshape.1671), calls=%async_computation.1 | async-start | bytes 655360 | tf_op jit(solution)/shard_map/all_to_all | solution.py:100
  202.7 31.0 %collective-permute-start = (bf16[2,6,10240]{2,0,1:T(2,128)(2,1)S(1)}, bf16[2,6,10240]{2,0,1:T(2,128)(2,1)S(1)}, u32[]{:S(2)}, u32[]{:S(2)}) collective-permute-start(bf16[2,6,10240]{2,0,1:T(2,128)(2,1)S(1)} %add_convert_fusion.5), channel_id=1, source_target_pairs={{8,0},{16,8},{24,16},{9,1},{17,9},{25,17},{10,2},{18,10},{26,18},{... | collective-permute-start | bytes 737288 | tf_op jit(solution)/shard_map/ppermute | solution.py:12
  205.1 23.7 %copy-start.170 = (f32[128,128]{1,0:T(8,128)S(1)}, f32[128,128]{1,0:T(8,128)}, u32[]{:S(2)}) copy-start(f32[128,128]{1,0:T(8,128)} %convolution_bitcast_fusion.43) | copy-start | bytes 196612
  205.1 24.4 %copy-start.166 = (f32[128,128]{1,0:T(8,128)S(1)}, f32[128,128]{1,0:T(8,128)}, u32[]{:S(2)}) copy-start(f32[128,128]{1,0:T(8,128)} %convolution_bitcast_fusion.42) | copy-start | bytes 196612
  205.1 25.1 %copy-start.162 = (f32[128,128]{1,0:T(8,128)S(1)}, f32[128,128]{1,0:T(8,128)}, u32[]{:S(2)}) copy-start(f32[128,128]{1,0:T(8,128)} %convolution_bitcast_fusion.41) | copy-start | bytes 196612
  205.1 25.7 %copy-start.158 = (f32[128,128]{1,0:T(8,128)S(1)}, f32[128,128]{1,0:T(8,128)}, u32[]{:S(2)}) copy-start(f32[128,128]{1,0:T(8,128)} %convolution_bitcast_fusion.40) | copy-start | bytes 196612
  205.1 26.4 %copy-start.154 = (f32[128,128]{1,0:T(8,128)S(1)}, f32[128,128]{1,0:T(8,128)}, u32[]{:S(2)}) copy-start(f32[128,128]{1,0:T(8,128)} %convolution_bitcast_fusion.39) | copy-start | bytes 196612
  205.1 27.1 %copy-start.150 = (f32[128,128]{1,0:T(8,128)S(1)}, f32[128,128]{1,0:T(8,128)}, u32[]{:S(2)}) copy-start(f32[128,128]{1,0:T(8,128)} %convolution_bitcast_fusion.38) | copy-start | bytes 196612
  205.1 27.8 %copy-start.149 = (f32[128,128]{1,0:T(8,128)S(1)}, f32[128,128]{1,0:T(8,128)}, u32[]{:S(2)}) copy-start(f32[128,128]{1,0:T(8,128)} %convolution_bitcast_fusion.37) | copy-start | bytes 196612
  225.4 26.6 %all-to-all-start.10 = ((bf16[4,2,15360]{2,1,0:T(2,128)(2,1)}), bf16[4,2,15360]{2,1,0:T(2,128)(2,1)S(1)}, u32[]{:S(2)}, u32[]{:S(2)}) async-start(bf16[4,2,15360]{2,1,0:T(2,128)(2,1)} %reshape.1695), calls=%async_computation.10 | async-start | bytes 491520 | tf_op jit(solution)/shard_map/all_to_all | solution.py:96
  252.0 31.3 %all-to-all-start.2 = ((bf16[4,2,15360]{2,1,0:T(2,128)(2,1)}), bf16[4,2,15360]{2,1,0:T(2,128)(2,1)S(1)}, u32[]{:S(2)}, u32[]{:S(2)}) async-start(bf16[4,2,15360]{2,1,0:T(2,128)(2,1)} %reshape.1687), calls=%async_computation.2 | async-start | bytes 491520 | tf_op jit(solution)/shard_map/all_to_all | solution.py:95
  314.8 10.0 %all-to-all-start.3 = ((bf16[8,6,2560]{2,1,0:T(8,128)(2,1)}), bf16[8,6,2560]{2,1,0:T(8,128)(2,1)}, u32[]{:S(2)}, u32[]{:S(2)}) async-start(bf16[8,6,2560]{2,1,0:T(8,128)(2,1)} %reshape.1681), calls=%async_computation.3 | async-start | bytes 655360 | tf_op jit(solution)/shard_map/all_to_all | solution.py:100
  364.0 22.6 %copy-start.105 = (bf16[2,6,10240]{2,0,1:T(2,128)(2,1)}, bf16[2,6,10240]{2,0,1:T(2,128)(2,1)S(1)}, u32[]{:S(2)}) copy-start(bf16[2,6,10240]{2,0,1:T(2,128)(2,1)S(1)} %add_convert_fusion.4) | copy-start | bytes 737284
  364.0 31.2 %collective-permute-start.1 = (bf16[2,6,10240]{2,0,1:T(2,128)(2,1)S(1)}, bf16[2,6,10240]{2,0,1:T(2,128)(2,1)S(1)}, u32[]{:S(2)}, u32[]{:S(2)}) collective-permute-start(bf16[2,6,10240]{2,0,1:T(2,128)(2,1)S(1)} %add_convert_fusion.4), channel_id=1, source_target_pairs={{8,0},{16,8},{24,16},{9,1},{17,9},{25,17},{10,2},{18,10},{26,18},{... | collective-permute-start | bytes 737288 | tf_op jit(solution)/shard_map/ppermute | solution.py:12
  366.4 24.0 %copy-start.172 = (f32[128,128]{1,0:T(8,128)S(1)}, f32[128,128]{1,0:T(8,128)}, u32[]{:S(2)}) copy-start(f32[128,128]{1,0:T(8,128)} %convolution_bitcast_fusion.34) | copy-start | bytes 196612
  366.4 25.4 %copy-start.167 = (f32[128,128]{1,0:T(8,128)S(1)}, f32[128,128]{1,0:T(8,128)}, u32[]{:S(2)}) copy-start(f32[128,128]{1,0:T(8,128)} %convolution_bitcast_fusion.32) | copy-start | bytes 196612
  366.4 26.1 %copy-start.163 = (f32[128,128]{1,0:T(8,128)S(1)}, f32[128,128]{1,0:T(8,128)}, u32[]{:S(2)}) copy-start(f32[128,128]{1,0:T(8,128)} %convolution_bitcast_fusion.31) | copy-start | bytes 196612
  366.4 26.8 %copy-start.159 = (f32[128,128]{1,0:T(8,128)S(1)}, f32[128,128]{1,0:T(8,128)}, u32[]{:S(2)}) copy-start(f32[128,128]{1,0:T(8,128)} %convolution_bitcast_fusion.30) | copy-start | bytes 196612
  366.4 27.4 %copy-start.155 = (f32[128,128]{1,0:T(8,128)S(1)}, f32[128,128]{1,0:T(8,128)}, u32[]{:S(2)}) copy-start(f32[128,128]{1,0:T(8,128)} %convolution_bitcast_fusion.29) | copy-start | bytes 196612
  366.4 28.1 %copy-start.151 = (f32[128,128]{1,0:T(8,128)S(1)}, f32[128,128]{1,0:T(8,128)}, u32[]{:S(2)}) copy-start(f32[128,128]{1,0:T(8,128)} %convolution_bitcast_fusion.28) | copy-start | bytes 196612
  386.6 26.9 %all-to-all-start.11 = ((bf16[4,2,15360]{2,1,0:T(2,128)(2,1)}), bf16[4,2,15360]{2,1,0:T(2,128)(2,1)S(1)}, u32[]{:S(2)}, u32[]{:S(2)}) async-start(bf16[4,2,15360]{2,1,0:T(2,128)(2,1)} %reshape.1697), calls=%async_computation.11 | async-start | bytes 491520 | tf_op jit(solution)/shard_map/all_to_all | solution.py:96
  413.6 31.1 %all-to-all-start.4 = ((bf16[4,2,15360]{2,1,0:T(2,128)(2,1)}), bf16[4,2,15360]{2,1,0:T(2,128)(2,1)S(1)}, u32[]{:S(2)}, u32[]{:S(2)}) async-start(bf16[4,2,15360]{2,1,0:T(2,128)(2,1)} %reshape.1689), calls=%async_computation.4 | async-start | bytes 491520 | tf_op jit(solution)/shard_map/all_to_all | solution.py:95
  476.2 10.0 %all-to-all-start.5 = ((bf16[8,6,2560]{2,1,0:T(8,128)(2,1)}), bf16[8,6,2560]{2,1,0:T(8,128)(2,1)}, u32[]{:S(2)}, u32[]{:S(2)}) async-start(bf16[8,6,2560]{2,1,0:T(8,128)(2,1)} %reshape.1682), calls=%async_computation.5 | async-start | bytes 655360 | tf_op jit(solution)/shard_map/all_to_all | solution.py:100
  523.5 30.9 %collective-permute-start.2 = (bf16[2,6,10240]{2,0,1:T(2,128)(2,1)S(1)}, bf16[2,6,10240]{2,0,1:T(2,128)(2,1)S(1)}, u32[]{:S(2)}, u32[]{:S(2)}) collective-permute-start(bf16[2,6,10240]{2,0,1:T(2,128)(2,1)S(1)} %add_convert_fusion.3), channel_id=1, source_target_pairs={{8,0},{16,8},{24,16},{9,1},{17,9},{25,17},{10,2},{18,10},{26,18},{... | collective-permute-start | bytes 737288 | tf_op jit(solution)/shard_map/ppermute | solution.py:12
  525.7 23.8 %copy-start.173 = (f32[128,128]{1,0:T(8,128)S(1)}, f32[128,128]{1,0:T(8,128)}, u32[]{:S(2)}) copy-start(f32[128,128]{1,0:T(8,128)} %convolution_bitcast_fusion.25) | copy-start | bytes 196612
  525.7 25.2 %copy-start.169 = (f32[128,128]{1,0:T(8,128)S(1)}, f32[128,128]{1,0:T(8,128)}, u32[]{:S(2)}) copy-start(f32[128,128]{1,0:T(8,128)} %convolution_bitcast_fusion.23) | copy-start | bytes 196612
  525.7 25.9 %copy-start.165 = (f32[128,128]{1,0:T(8,128)S(1)}, f32[128,128]{1,0:T(8,128)}, u32[]{:S(2)}) copy-start(f32[128,128]{1,0:T(8,128)} %convolution_bitcast_fusion.22) | copy-start | bytes 196612
  525.7 26.6 %copy-start.161 = (f32[128,128]{1,0:T(8,128)S(1)}, f32[128,128]{1,0:T(8,128)}, u32[]{:S(2)}) copy-start(f32[128,128]{1,0:T(8,128)} %convolution_bitcast_fusion.21) | copy-start | bytes 196612
  525.7 27.2 %copy-start.157 = (f32[128,128]{1,0:T(8,128)S(1)}, f32[128,128]{1,0:T(8,128)}, u32[]{:S(2)}) copy-start(f32[128,128]{1,0:T(8,128)} %convolution_bitcast_fusion.20) | copy-start | bytes 196612
  525.7 27.9 %copy-start.153 = (f32[128,128]{1,0:T(8,128)S(1)}, f32[128,128]{1,0:T(8,128)}, u32[]{:S(2)}) copy-start(f32[128,128]{1,0:T(8,128)} %convolution_bitcast_fusion.19) | copy-start | bytes 196612
  545.9 26.8 %all-to-all-start.12 = ((bf16[4,2,15360]{2,1,0:T(2,128)(2,1)}), bf16[4,2,15360]{2,1,0:T(2,128)(2,1)S(1)}, u32[]{:S(2)}, u32[]{:S(2)}) async-start(bf16[4,2,15360]{2,1,0:T(2,128)(2,1)} %reshape.1699), calls=%async_computation.12 | async-start | bytes 491520 | tf_op jit(solution)/shard_map/all_to_all | solution.py:96
  572.7 31.3 %all-to-all-start.6 = ((bf16[4,2,15360]{2,1,0:T(2,128)(2,1)}), bf16[4,2,15360]{2,1,0:T(2,128)(2,1)S(1)}, u32[]{:S(2)}, u32[]{:S(2)}) async-start(bf16[4,2,15360]{2,1,0:T(2,128)(2,1)} %reshape.1691), calls=%async_computation.6 | async-start | bytes 491520 | tf_op jit(solution)/shard_map/all_to_all | solution.py:95
  635.5 10.2 %all-to-all-start.7 = ((bf16[8,6,2560]{2,1,0:T(8,128)(2,1)}), bf16[8,6,2560]{2,1,0:T(8,128)(2,1)}, u32[]{:S(2)}, u32[]{:S(2)}) async-start(bf16[8,6,2560]{2,1,0:T(8,128)(2,1)} %reshape.1683), calls=%async_computation.7 | async-start | bytes 655360 | tf_op jit(solution)/shard_map/all_to_all | solution.py:100
  685.6 27.1 %collective-permute-start.3 = (bf16[2,6,10240]{2,0,1:T(2,128)(2,1)S(1)}, bf16[2,6,10240]{2,0,1:T(2,128)(2,1)S(1)}, u32[]{:S(2)}, u32[]{:S(2)}) collective-permute-start(bf16[2,6,10240]{2,0,1:T(2,128)(2,1)S(1)} %add_convert_fusion.2), channel_id=1, source_target_pairs={{8,0},{16,8},{24,16},{9,1},{17,9},{25,17},{10,2},{18,10},{26,18},{... | collective-permute-start | bytes 737288 | tf_op jit(solution)/shard_map/ppermute | solution.py:12
  687.5 23.8 %copy-start.121 = (f32[9,64,64]{2,1,0:T(8,128)S(1)}, f32[9,64,64]{2,1,0:T(8,128)}, u32[]{:S(2)}) copy-start(f32[9,64,64]{2,1,0:T(8,128)} %constant_dynamic-update-slice_fusion.35) | copy-start | bytes 442372
  687.5 24.6 %copy-start.171 = (f32[128,128]{1,0:T(8,128)S(1)}, f32[128,128]{1,0:T(8,128)}, u32[]{:S(2)}) copy-start(f32[128,128]{1,0:T(8,128)} %convolution_bitcast_fusion.15) | copy-start | bytes 196612
  687.5 24.7 %copy-start.168 = (f32[128,128]{1,0:T(8,128)S(1)}, f32[128,128]{1,0:T(8,128)}, u32[]{:S(2)}) copy-start(f32[128,128]{1,0:T(8,128)} %convolution_bitcast_fusion.14) | copy-start | bytes 196612
  687.5 24.7 %copy-start.164 = (f32[128,128]{1,0:T(8,128)S(1)}, f32[128,128]{1,0:T(8,128)}, u32[]{:S(2)}) copy-start(f32[128,128]{1,0:T(8,128)} %convolution_bitcast_fusion.13) | copy-start | bytes 196612
  687.6 24.8 %copy-start.160 = (f32[128,128]{1,0:T(8,128)S(1)}, f32[128,128]{1,0:T(8,128)}, u32[]{:S(2)}) copy-start(f32[128,128]{1,0:T(8,128)} %convolution_bitcast_fusion.12) | copy-start | bytes 196612
  687.6 24.9 %copy-start.156 = (f32[128,128]{1,0:T(8,128)S(1)}, f32[128,128]{1,0:T(8,128)}, u32[]{:S(2)}) copy-start(f32[128,128]{1,0:T(8,128)} %convolution_bitcast_fusion.11) | copy-start | bytes 196612
  687.6 25.0 %copy-start.152 = (f32[128,128]{1,0:T(8,128)S(1)}, f32[128,128]{1,0:T(8,128)}, u32[]{:S(2)}) copy-start(f32[128,128]{1,0:T(8,128)} %convolution_bitcast_fusion.10) | copy-start | bytes 196612
  707.7 23.3 %all-to-all-start.13 = ((bf16[4,2,15360]{2,1,0:T(2,128)(2,1)}), bf16[4,2,15360]{2,1,0:T(2,128)(2,1)S(1)}, u32[]{:S(2)}, u32[]{:S(2)}) async-start(bf16[4,2,15360]{2,1,0:T(2,128)(2,1)} %reshape.1701), calls=%async_computation.13 | async-start | bytes 491520 | tf_op jit(solution)/shard_map/all_to_all | solution.py:96
  731.0 31.1 %all-to-all-start.8 = ((bf16[4,2,15360]{2,1,0:T(2,128)(2,1)}), bf16[4,2,15360]{2,1,0:T(2,128)(2,1)S(1)}, u32[]{:S(2)}, u32[]{:S(2)}) async-start(bf16[4,2,15360]{2,1,0:T(2,128)(2,1)} %reshape.1693), calls=%async_computation.8 | async-start | bytes 491520 | tf_op jit(solution)/shard_map/all_to_all | solution.py:95
  735.9 24.8 %copy-start.122 = (f32[9,64,64]{2,1,0:T(8,128)}, f32[9,64,64]{2,1,0:T(8,128)S(1)}, u32[]{:S(2)}) copy-start(f32[9,64,64]{2,1,0:T(8,128)S(1)} %get-tuple-element.143) | copy-start | bytes 442372
  788.7 9.9 %all-to-all-start.9 = ((bf16[8,6,2560]{2,1,0:T(8,128)(2,1)}), bf16[8,6,2560]{2,1,0:T(8,128)(2,1)S(1)}, u32[]{:S(2)}, u32[]{:S(2)}) async-start(bf16[8,6,2560]{2,1,0:T(8,128)(2,1)} %reshape.1684), calls=%async_computation.9 | async-start | bytes 655360 | tf_op jit(solution)/shard_map/all_to_all | solution.py:100
  793.0 127.7 %all-reduce.17.cloned.1.call-start = ((), (), s32[]{:S(2)}) async-start(), calls=%async_computation.15 | async-start | bytes 589824 | tf_op jit(solution)/shard_map/psum | solution.py:134
  841.0 24.0 %copy-start.53 = (bf16[2,6,10240]{2,0,1:T(2,128)(2,1)S(1)}, bf16[2,6,10240]{2,0,1:T(2,128)(2,1)}, u32[]{:S(2)}) copy-start(bf16[2,6,10240]{2,0,1:T(2,128)(2,1)} %fusion.25) | copy-start | bytes 737284
  841.1 24.0 %copy-start.106 = (bf16[2,6,10240]{2,0,1:T(2,128)(2,1)S(1)}, bf16[2,6,10240]{2,0,1:T(2,128)(2,1)}, u32[]{:S(2)}) copy-start(bf16[2,6,10240]{2,0,1:T(2,128)(2,1)} %copy-done.105) | copy-start | bytes 737284
  841.1 24.0 %copy-start.108 = (bf16[2,6,10240]{2,0,1:T(2,128)(2,1)S(1)}, bf16[2,6,10240]{2,0,1:T(2,128)(2,1)}, u32[]{:S(2)}) copy-start(bf16[2,6,10240]{2,0,1:T(2,128)(2,1)} %copy-done.107) | copy-start | bytes 737284
  841.1 24.0 %copy-start.110 = (bf16[2,6,10240]{2,0,1:T(2,128)(2,1)S(1)}, bf16[2,6,10240]{2,0,1:T(2,128)(2,1)}, u32[]{:S(2)}) copy-start(bf16[2,6,10240]{2,0,1:T(2,128)(2,1)} %copy-done.109) | copy-start | bytes 737284
  841.1 24.0 %copy-start.174 = (pred[2]{0:T(512)(128)(4,1)S(1)}, pred[2]{0:T(512)(128)(4,1)}, u32[]{:S(2)}) copy-start(pred[2]{0:T(512)(128)(4,1)} %get-tuple-element.138) | copy-start | bytes 10
  841.1 24.0 %copy-start.175 = (pred[2]{0:T(512)(128)(4,1)S(1)}, pred[2]{0:T(512)(128)(4,1)}, u32[]{:S(2)}) copy-start(pred[2]{0:T(512)(128)(4,1)} %get-tuple-element.139) | copy-start | bytes 10
  841.1 24.0 %copy-start.176 = (pred[2]{0:T(512)(128)(4,1)S(1)}, pred[2]{0:T(512)(128)(4,1)}, u32[]{:S(2)}) copy-start(pred[2]{0:T(512)(128)(4,1)} %get-tuple-element.136) | copy-start | bytes 10
  841.1 24.0 %copy-start.177 = (pred[2]{0:T(512)(128)(4,1)S(1)}, pred[2]{0:T(512)(128)(4,1)}, u32[]{:S(2)}) copy-start(pred[2]{0:T(512)(128)(4,1)} %get-tuple-element.137) | copy-start | bytes 10
  841.1 24.0 %copy-start.178 = (pred[2]{0:T(512)(128)(4,1)S(1)}, pred[2]{0:T(512)(128)(4,1)}, u32[]{:S(2)}) copy-start(pred[2]{0:T(512)(128)(4,1)} %iota_compare_fusion.4) | copy-start | bytes 10
  861.3 9.1 all-to-all-start.14
  (135 other events, 1551.2 us)
Sparse Core Ops, SparseCore 0:
  820.6 53.1 all-reduce.16
where the time goes:
time: 944 us; the launch traced here: 930 us
  local copies, waits for them, and re-layouts  609 us (65%)
  matrix products  137 us (15%)
  starting transfers between devices  70 us (7%)
  other arithmetic  49 us (5%)
  blocking collectives  23.7 us (3%)
  waiting for transfers between devices  23.2 us (2%)
  between operations  17.9 us (2%)
    unnamed x379, local copies, waits for them, and re-layouts  229 us
    reshape x105, local copies, waits for them, and re-layouts, split_pixels(): return a.reshape(a.shape[:-1] + (a.shape[-1] // chans, chans))  112 us
    all_to_all x10, local copies, waits for them, and re-layouts, section_backward(): lax.all_to_all(h, 'tm', split_axis=2, concat_axis=0, tiled=True)  61.8 us
    dot_general x45, matrix products, spatial_back(): jnp.einsum('nrpa,nrpb->ab', xpiece, gz_pairs, preferred_element_type=jnp....  54.5 us
    all_to_all x10, local copies, waits for them, and re-layouts, section_backward(): lax.all_to_all(gradient_piece, 'tm', split_axis=2, concat_axis=0, tiled=T...  52.1 us
    convert_element_type x5, local copies, waits for them, and re-layouts, section_backward(): h = (z * sig).astype(jnp.bfloat16)  51.3 us
    select_n x5, local copies, waits for them, and re-layouts, body(): incoming = jnp.where(section_idx == number_sections - 1, top_grad, received)  40.8 us
    dot_general x45, matrix products, spatial_fwd(): jnp.einsum('nrpa,ab->nrpb', piece, paired_kernel(ws[3 * i + j]), preferre...  28.6 us
  transfers between devices with their start and end apart: 20, of which 6 were waited for; matrix products, arithmetic and copies ran while one was open for 48% of the time, Pallas kernels for 0%

commit v1 on v0

--- a/solution.py
+++ b/solution.py
@@ -91,8 +91,31 @@
     sig = jax.nn.sigmoid(z)
     h = (z * sig).astype(jnp.bfloat16)
     deriv = sig * (1.0 + z * (1.0 - sig))
+
+    def press_the_pieces_all(my_tile, link_axis):
+        top = lax.axis_size(link_axis)
+        ready = lax.axis_index(link_axis)
+        y2, o_now = (top, ready)
+        spare = my_tile.shape[2] // y2
+        w2 = list(my_tile.shape)
+        w2[2] = spare
+        tall = w2[0]
+        w2[0] = tall * y2
+        value_now = jnp.zeros(w2, my_tile.dtype)
+        for dev_i in range(y2):
+            latest = lax.dynamic_slice_in_dim(my_tile, (o_now ^ dev_i) * spare, spare, axis=2)
+            if dev_i:
+                r_now = range(y2)
+                part_now = map(lambda pp: (pp, pp ^ dev_i), r_now)
+                wide_out = list(part_now)
+                latest = lax.ppermute(latest, link_axis, wide_out)
+            value_now = lax.dynamic_update_slice_in_dim(
+                value_now, latest, (o_now ^ dev_i) * tall, axis=0
+            )
+        return value_now
+
     tile_gradient, h_tile = (
-        lax.all_to_all(gradient_piece, "tm", split_axis=2, concat_axis=0, tiled=True),
+        press_the_pieces_all(gradient_piece, "tm"),
         lax.all_to_all(h, "tm", split_axis=2, concat_axis=0, tiled=True),
     )
     gradient_padded = jnp.pad(tile_gradient, ((dilation_step, dilation_step), (0, 0), (0, 0)))

time: 944 us -> 769 us (0.81)
  local copies, waits for them, and re-layouts: 609 us -> 413 us
  waiting for transfers between devices: 23.2 us -> 42.1 us
    unnamed x379 -> x339, local copies, waits for them, and re-layouts: 229 us -> 116 us
    all_to_all x10 -> x0, local copies, waits for them, and re-layouts: 52.1 us -> none  [section_backward(): lax.all_to_all(gradient_piece, 'tm', split_axis=2, concat_axis=0, tiled=T...]
    select_n x5 -> x0, local copies, waits for them, and re-layouts: 40.8 us -> none  [body(): incoming = jnp.where(section_idx == number_sections - 1, top_grad, received)]
    all_to_all x5 -> x0, starting transfers between devices: 20.8 us -> none  [section_backward(): lax.all_to_all(gradient_piece, 'tm', split_axis=2, concat_axis=0, tiled=T...]
    ppermute x0 -> x15, starting transfers between devices: none -> 17.7 us  [press_the_pieces_all(): latest = lax.ppermute(latest, link_axis, wide_out)]
    ppermute x0 -> x15, waiting for transfers between devices: none -> 14.7 us  [press_the_pieces_all(): latest = lax.ppermute(latest, link_axis, wide_out)]
  transfers between devices with their start and end apart: 20 -> 30, of which waited for: 6 -> 14; matrix products, arithmetic and copies ran while one was open for 48% -> 50% of each run, Pallas kernels for 0% -> 0%
where the time goes in v1:
time: 769 us; the launch traced here: 754 us
  local copies, waits for them, and re-layouts  413 us (54%)
  matrix products  146 us (19%)
  starting transfers between devices  64.8 us (8%)
  other arithmetic  46.4 us (6%)
  waiting for transfers between devices  42.1 us (5%)
  blocking collectives  23.7 us (3%)
  between operations  17.9 us (2%)
    unnamed x339, local copies, waits for them, and re-layouts  116 us
    reshape x105, local copies, waits for them, and re-layouts, split_pixels(): return a.reshape(a.shape[:-1] + (a.shape[-1] // chans, chans))  113 us
    all_to_all x10, local copies, waits for them, and re-layouts, section_backward(): lax.all_to_all(h, 'tm', split_axis=2, concat_axis=0, tiled=True)  61.8 us
    dot_general x45, matrix products, spatial_back(): jnp.einsum('nrpa,nrpb->ab', xpiece, gz_pairs, preferred_element_type=jnp....  60.6 us
    convert_element_type x5, local copies, waits for them, and re-layouts, section_backward(): h = (z * sig).astype(jnp.bfloat16)  51.2 us
    dot_general x45, matrix products, spatial_fwd(): jnp.einsum('nrpa,ab->nrpb', piece, paired_kernel(ws[3 * i + j]), preferre...  30.1 us
    dot_general x45, matrix products, spatial_back(): jnp.einsum('nrpb,ab->nrpa', gpiece, paired_kernel(ws[3 * i + j]), preferr...  28.4 us
    unnamed x40, other arithmetic  24.2 us
  transfers between devices with their start and end apart: 30, of which 14 were waited for; matrix products, arithmetic and copies ran while one was open for 50% of the time, Pallas kernels for 0%

profile of v1, /device:TPU:24, one launch (start us, length us, event | category | flops | bytes accessed | tf_op | source)
XLA Modules:
  0.0 754.0 jit_solution(12272145761379048959)
XLA Ops:
  9.8 2.4 collective-permute-start.2
  16.4 2.3 constant_dynamic-slice_fusion
  22.3 3.2 pad_slice_fusion.34
  33.5 3.0 pad_slice_fusion.82
  45.0 3.0 pad_slice_fusion.66
  59.0 3.0 pad_slice_fusion.50
  74.1 3.6 pad_slice_fusion.18
  117.3 3.9 all-to-all-start
  122.3 4.5 all-to-all-done
  128.1 2.4 multiply_convert_fusion.13
  151.5 2.9 pad_slice_fusion.74
  170.4 2.4 collective-permute-start.3
  172.9 10.3 %copy.790 = bf16[2,6,10240]{1,0,2:T(2,128)(2,1)} copy(bf16[2,6,10240]{2,0,1:T(2,128)(2,1)} %get-tuple-element.11) | data formatting | bytes 491520 | tf_op jit(solution)/shard_map/convert_element_type | solution.py:92
  183.2 9.9 %reshape.1687 = bf16[4,2,15360]{2,1,0:T(2,128)(2,1)} reshape(bf16[10240,2,6]{2,1,0:T(2,128)(2,1)} %bitcast.1139) | data formatting | bytes 491520
  193.1 3.8 all-to-all-start.5
  202.2 12.7 %reshape.1688 = bf16[10240,2,6]{2,1,0:T(2,128)(2,1)} reshape(bf16[4,2,15360]{2,1,0:T(2,128)(2,1)S(1)} %all-to-all-done.5) | data formatting | bytes 491520
  214.9 12.2 %copy.883 = bf16[2,6,4,2560]{3,2,0,1:T(4,128)(2,1)S(1)} copy(bf16[2,6,4,2560]{1,0,3,2:T(2,128)(2,1)} %bitcast.1140) | data formatting | bytes 491520 | tf_op jit(solution)/shard_map/all_to_all | solution.py:119
  232.7 3.7 collective-permute-done.5
  244.1 2.1 reshape.1683
  246.2 4.1 all-to-all-start.1
  252.1 3.8 all-to-all-done.1
  260.1 1.9 convolution_bitcast_fusion.27
  275.9 3.0 pad_slice_fusion.58
  295.8 2.4 collective-permute-start.7
  298.2 10.2 %copy.793 = bf16[2,6,10240]{1,0,2:T(2,128)(2,1)} copy(bf16[2,6,10240]{2,0,1:T(2,128)(2,1)} %get-tuple-element.9) | data formatting | bytes 491520 | tf_op jit(solution)/shard_map/convert_element_type | solution.py:92
  308.4 9.9 %reshape.1689 = bf16[4,2,15360]{2,1,0:T(2,128)(2,1)} reshape(bf16[10240,2,6]{2,1,0:T(2,128)(2,1)} %bitcast.1141) | data formatting | bytes 491520
  318.3 3.6 all-to-all-start.6
  327.2 12.7 %reshape.1690 = bf16[10240,2,6]{2,1,0:T(2,128)(2,1)} reshape(bf16[4,2,15360]{2,1,0:T(2,128)(2,1)S(1)} %all-to-all-done.6) | data formatting | bytes 491520
  339.9 12.2 %copy.884 = bf16[2,6,4,2560]{3,2,0,1:T(4,128)(2,1)S(1)} copy(bf16[2,6,4,2560]{1,0,3,2:T(2,128)(2,1)} %bitcast.1142) | data formatting | bytes 491520 | tf_op jit(solution)/shard_map/all_to_all | solution.py:119
  357.7 3.4 collective-permute-done.9
  367.7 2.1 reshape.1684
  369.8 4.1 all-to-all-start.2
  375.7 3.8 all-to-all-done.2
  383.7 1.9 convolution_bitcast_fusion.18
  399.5 3.0 pad_slice_fusion.42
  419.4 2.4 collective-permute-start.11
  421.8 10.3 %copy.796 = bf16[2,6,10240]{1,0,2:T(2,128)(2,1)} copy(bf16[2,6,10240]{2,0,1:T(2,128)(2,1)} %get-tuple-element.7) | data formatting | bytes 491520 | tf_op jit(solution)/shard_map/convert_element_type | solution.py:92
  432.1 9.9 %reshape.1691 = bf16[4,2,15360]{2,1,0:T(2,128)(2,1)} reshape(bf16[10240,2,6]{2,1,0:T(2,128)(2,1)} %bitcast.1143) | data formatting | bytes 491520
  442.0 3.8 all-to-all-start.7
  451.1 12.7 %reshape.1692 = bf16[10240,2,6]{2,1,0:T(2,128)(2,1)} reshape(bf16[4,2,15360]{2,1,0:T(2,128)(2,1)S(1)} %all-to-all-done.7) | data formatting | bytes 491520
  463.8 12.2 %copy.885 = bf16[2,6,4,2560]{3,2,0,1:T(4,128)(2,1)S(1)} copy(bf16[2,6,4,2560]{1,0,3,2:T(2,128)(2,1)} %bitcast.1144) | data formatting | bytes 491520 | tf_op jit(solution)/shard_map/all_to_all | solution.py:119
  481.6 3.8 collective-permute-done.13
  492.0 2.1 reshape.1685
  494.1 4.1 all-to-all-start.3
  500.0 3.8 all-to-all-done.3
  508.0 1.9 convolution_bitcast_fusion.9
  523.8 3.0 pad_slice_fusion.26
  545.6 10.2 %copy.799 = bf16[2,6,10240]{1,0,2:T(2,128)(2,1)} copy(bf16[2,6,10240]{2,0,1:T(2,128)(2,1)} %get-tuple-element.5) | data formatting | bytes 491520 | tf_op jit(solution)/shard_map/convert_element_type | solution.py:92
  555.8 9.9 %reshape.1693 = bf16[4,2,15360]{2,1,0:T(2,128)(2,1)} reshape(bf16[10240,2,6]{2,1,0:T(2,128)(2,1)} %bitcast.1145) | data formatting | bytes 491520
  565.7 3.6 all-to-all-start.8
  574.6 12.7 %reshape.1694 = bf16[10240,2,6]{2,1,0:T(2,128)(2,1)} reshape(bf16[4,2,15360]{2,1,0:T(2,128)(2,1)S(1)} %all-to-all-done.8) | data formatting | bytes 491520
  587.3 12.2 %copy.886 = bf16[2,6,4,2560]{3,2,0,1:T(4,128)(2,1)S(1)} copy(bf16[2,6,4,2560]{1,0,3,2:T(2,128)(2,1)} %bitcast.1146) | data formatting | bytes 491520 | tf_op jit(solution)/shard_map/all_to_all | solution.py:119
  605.1 3.7 collective-permute-done.17
  614.0 3.6 all-to-all-start.4
  619.5 3.6 all-to-all-done.4
  643.0 2.0 add_bitcast_fusion
  646.7 3.2 pad_slice_fusion.10
  665.8 10.2 %copy.802 = bf16[2,6,10240]{1,0,2:T(2,128)(2,1)} copy(bf16[2,6,10240]{2,0,1:T(2,128)(2,1)} %get-tuple-element.3) | data formatting | bytes 491520 | tf_op jit(solution)/shard_map/convert_element_type | solution.py:92
  676.1 9.9 %reshape.1695 = bf16[4,2,15360]{2,1,0:T(2,128)(2,1)} reshape(bf16[10240,2,6]{2,1,0:T(2,128)(2,1)} %bitcast.1147) | data formatting | bytes 491520
  686.0 3.4 all-to-all-start.9
  691.2 3.6 all-to-all-done.9
  694.8 12.7 %reshape.1696 = bf16[10240,2,6]{2,1,0:T(2,128)(2,1)} reshape(bf16[4,2,15360]{2,1,0:T(2,128)(2,1)S(1)} %all-to-all-done.9) | data formatting | bytes 491520
  707.6 12.3 %copy.887 = bf16[2,6,4,2560]{3,2,0,1:T(4,128)(2,1)S(1)} copy(bf16[2,6,4,2560]{1,0,3,2:T(2,128)(2,1)} %bitcast.1148) | data formatting | bytes 491520 | tf_op jit(solution)/shard_map/all_to_all | solution.py:119
  721.5 23.7 %psum.15 = f32[1,3,64,64]{3,2,1,0:T(8,128)} all-reduce(f32[1,3,64,64]{3,2,1,0:T(8,128)S(1)} %fusion.173), channel_id=1, replica_groups=mesh['section'=4,'tm'=4,'batch'=2] {'tm','batch'}, use_global_device_ids=true, to_apply=%region_1.2 | all-reduce | flops 12288 | bytes 98304 | tf_op jit(solution)/shard_map/psum | solution.py:157
  (787 shorter events, 352.5 us)
Async XLA Ops:
  9.8 104.5 %collective-permute-start.2 = (bf16[2,6,2560]{2,0,1:T(2,128)(2,1)S(1)}, bf16[2,6,2560]{2,0,1:T(2,128)(2,1)S(1)}, u32[]{:S(2)}, u32[]{:S(2)}) collective-permute-start(bf16[2,6,2560]{2,0,1:T(2,128)(2,1)S(1)} %get-tuple-element.124), channel_id=1, source_target_pairs={{0,6},{2,4},{4,2},{6,0},{1,7},{3,5},{5,3},{7,1},{8,14},{10,12},{12... | collective-permute-start | bytes 184328 | tf_op jit(solution)/shard_map/ppermute | solution.py:111
  12.3 101.1 %collective-permute-start.1 = (bf16[2,6,2560]{2,0,1:T(2,128)(2,1)}, bf16[2,6,2560]{2,0,1:T(2,128)(2,1)}, u32[]{:S(2)}, u32[]{:S(2)}) collective-permute-start(bf16[2,6,2560]{2,0,1:T(2,128)(2,1)} %get-tuple-element.125), channel_id=1, source_target_pairs={{0,4},{2,6},{4,0},{6,2},{1,5},{3,7},{5,1},{7,3},{8,12},{10,14},{12... | collective-permute-start | bytes 184328 | tf_op jit(solution)/shard_map/ppermute | solution.py:111
  12.8 99.7 %collective-permute-start = (bf16[2,6,2560]{2,0,1:T(2,128)(2,1)}, bf16[2,6,2560]{2,0,1:T(2,128)(2,1)}, u32[]{:S(2)}, u32[]{:S(2)}) collective-permute-start(bf16[2,6,2560]{2,0,1:T(2,128)(2,1)} %get-tuple-element.126), channel_id=1, source_target_pairs={{0,2},{2,0},{4,6},{6,4},{1,3},{3,1},{5,7},{7,5},{8,10},{10,8},{12,... | collective-permute-start | bytes 184328 | tf_op jit(solution)/shard_map/ppermute | solution.py:111
  15.6 146.6 %copy-start.16 = (bf16[128,128,1,1]{1,0,2,3:T(8,128)(2,1)}, bf16[128,128,1,1]{1,0,2,3:T(8,128)(2,1)S(1)}, u32[]{:S(2)}) copy-start(bf16[128,128,1,1]{1,0,2,3:T(8,128)(2,1)S(1)} %reshape.1605) | copy-start | bytes 98308
  15.7 146.8 %copy-start.11 = (bf16[128,128,1,1]{1,0,2,3:T(8,128)(2,1)}, bf16[128,128,1,1]{1,0,2,3:T(8,128)(2,1)S(1)}, u32[]{:S(2)}) copy-start(bf16[128,128,1,1]{1,0,2,3:T(8,128)(2,1)S(1)} %reshape.1606) | copy-start | bytes 98308
  15.8 146.9 %copy-start.6 = (bf16[128,128,1,1]{1,0,2,3:T(8,128)(2,1)}, bf16[128,128,1,1]{1,0,2,3:T(8,128)(2,1)S(1)}, u32[]{:S(2)}) copy-start(bf16[128,128,1,1]{1,0,2,3:T(8,128)(2,1)S(1)} %reshape.1607) | copy-start | bytes 98308
  15.9 148.0 %copy-start.1 = (bf16[128,128,1,1]{1,0,2,3:T(8,128)(2,1)}, bf16[128,128,1,1]{1,0,2,3:T(8,128)(2,1)S(1)}, u32[]{:S(2)}) copy-start(bf16[128,128,1,1]{1,0,2,3:T(8,128)(2,1)S(1)} %reshape.1608) | copy-start | bytes 98308
  16.3 145.6 %copy-start.21 = (bf16[128,128,1,1]{1,0,2,3:T(8,128)(2,1)}, bf16[128,128,1,1]{1,0,2,3:T(8,128)(2,1)S(1)}, u32[]{:S(2)}) copy-start(bf16[128,128,1,1]{1,0,2,3:T(8,128)(2,1)S(1)} %reshape.1604) | copy-start | bytes 98308
  18.9 91.4 %copy-start.41 = (bf16[2,6,80,128]{3,2,0,1:T(8,128)(2,1)}, bf16[2,6,80,128]{3,2,0,1:T(8,128)(2,1)S(1)}, u32[]{:S(2)}) copy-start(bf16[2,6,80,128]{3,2,0,1:T(8,128)(2,1)S(1)} %reshape.1506) | copy-start | bytes 737284
  117.3 9.4 %all-to-all-start = ((bf16[8,6,2560]{2,1,0:T(8,128)(2,1)}), bf16[8,6,2560]{2,1,0:T(8,128)(2,1)S(1)}, u32[]{:S(2)}, u32[]{:S(2)}) async-start(bf16[8,6,2560]{2,1,0:T(8,128)(2,1)} %reshape.1673), calls=%async_computation | async-start | bytes 655360 | tf_op jit(solution)/shard_map/all_to_all | solution.py:123
  170.4 57.1 %collective-permute-start.3 = (bf16[2,6,10240]{2,0,1:T(2,128)(2,1)S(1)}, bf16[2,6,10240]{2,0,1:T(2,128)(2,1)S(1)}, u32[]{:S(2)}, u32[]{:S(2)}) collective-permute-start(bf16[2,6,10240]{2,0,1:T(2,128)(2,1)S(1)} %fusion.6), channel_id=1, source_target_pairs={{8,0},{16,8},{24,16},{9,1},{17,9},{25,17},{10,2},{18,10},{26,18},{... | collective-permute-start | bytes 737288 | tf_op jit(solution)/shard_map/ppermute | solution.py:12
  172.9 24.1 %copy-start.160 = (f32[128,128]{1,0:T(8,128)S(1)}, f32[128,128]{1,0:T(8,128)}, u32[]{:S(2)}) copy-start(f32[128,128]{1,0:T(8,128)} %convolution_bitcast_fusion.43) | copy-start | bytes 196612
  172.9 24.8 %copy-start.158 = (f32[128,128]{1,0:T(8,128)S(1)}, f32[128,128]{1,0:T(8,128)}, u32[]{:S(2)}) copy-start(f32[128,128]{1,0:T(8,128)} %convolution_bitcast_fusion.42) | copy-start | bytes 196612
  172.9 25.4 %copy-start.154 = (f32[128,128]{1,0:T(8,128)S(1)}, f32[128,128]{1,0:T(8,128)}, u32[]{:S(2)}) copy-start(f32[128,128]{1,0:T(8,128)} %convolution_bitcast_fusion.41) | copy-start | bytes 196612
  172.9 26.1 %copy-start.150 = (f32[128,128]{1,0:T(8,128)S(1)}, f32[128,128]{1,0:T(8,128)}, u32[]{:S(2)}) copy-start(f32[128,128]{1,0:T(8,128)} %convolution_bitcast_fusion.40) | copy-start | bytes 196612
  172.9 26.8 %copy-start.146 = (f32[128,128]{1,0:T(8,128)S(1)}, f32[128,128]{1,0:T(8,128)}, u32[]{:S(2)}) copy-start(f32[128,128]{1,0:T(8,128)} %convolution_bitcast_fusion.39) | copy-start | bytes 196612
  172.9 27.5 %copy-start.142 = (f32[128,128]{1,0:T(8,128)S(1)}, f32[128,128]{1,0:T(8,128)}, u32[]{:S(2)}) copy-start(f32[128,128]{1,0:T(8,128)} %convolution_bitcast_fusion.38) | copy-start | bytes 196612
  172.9 28.1 %copy-start.141 = (f32[128,128]{1,0:T(8,128)S(1)}, f32[128,128]{1,0:T(8,128)}, u32[]{:S(2)}) copy-start(f32[128,128]{1,0:T(8,128)} %convolution_bitcast_fusion.37) | copy-start | bytes 196612
  193.1 9.1 %all-to-all-start.5 = ((bf16[4,2,15360]{2,1,0:T(2,128)(2,1)}), bf16[4,2,15360]{2,1,0:T(2,128)(2,1)S(1)}, u32[]{:S(2)}, u32[]{:S(2)}) async-start(bf16[4,2,15360]{2,1,0:T(2,128)(2,1)} %reshape.1687), calls=%async_computation.5 | async-start | bytes 491520 | tf_op jit(solution)/shard_map/all_to_all | solution.py:119
  228.1 4.5 collective-permute-start.4
  230.6 5.9 collective-permute-start.6
  232.1 4.3 collective-permute-start.5
  246.2 9.7 %all-to-all-start.1 = ((bf16[8,6,2560]{2,1,0:T(8,128)(2,1)}), bf16[8,6,2560]{2,1,0:T(8,128)(2,1)}, u32[]{:S(2)}, u32[]{:S(2)}) async-start(bf16[8,6,2560]{2,1,0:T(8,128)(2,1)} %reshape.1683), calls=%async_computation.1 | async-start | bytes 655360 | tf_op jit(solution)/shard_map/all_to_all | solution.py:123
  295.8 56.8 %collective-permute-start.7 = (bf16[2,6,10240]{2,0,1:T(2,128)(2,1)S(1)}, bf16[2,6,10240]{2,0,1:T(2,128)(2,1)S(1)}, u32[]{:S(2)}, u32[]{:S(2)}) collective-permute-start(bf16[2,6,10240]{2,0,1:T(2,128)(2,1)S(1)} %add_convert_fusion.3), channel_id=1, source_target_pairs={{8,0},{16,8},{24,16},{9,1},{17,9},{25,17},{10,2},{18,10},{26,18},{... | collective-permute-start | bytes 737288 | tf_op jit(solution)/shard_map/ppermute | solution.py:12
  298.1 23.8 %copy-start.115 = (f32[9,64,64]{2,1,0:T(8,128)S(1)}, f32[9,64,64]{2,1,0:T(8,128)}, u32[]{:S(2)}) copy-start(f32[9,64,64]{2,1,0:T(8,128)} %constant_dynamic-update-slice_fusion.17) | copy-start | bytes 442372
  298.2 26.3 %copy-start.155 = (f32[128,128]{1,0:T(8,128)S(1)}, f32[128,128]{1,0:T(8,128)}, u32[]{:S(2)}) copy-start(f32[128,128]{1,0:T(8,128)} %convolution_bitcast_fusion.31) | copy-start | bytes 196612
  298.2 26.4 %copy-start.151 = (f32[128,128]{1,0:T(8,128)S(1)}, f32[128,128]{1,0:T(8,128)}, u32[]{:S(2)}) copy-start(f32[128,128]{1,0:T(8,128)} %convolution_bitcast_fusion.30) | copy-start | bytes 196612
  298.2 26.5 %copy-start.147 = (f32[128,128]{1,0:T(8,128)S(1)}, f32[128,128]{1,0:T(8,128)}, u32[]{:S(2)}) copy-start(f32[128,128]{1,0:T(8,128)} %convolution_bitcast_fusion.29) | copy-start | bytes 196612
  298.2 26.5 %copy-start.143 = (f32[128,128]{1,0:T(8,128)S(1)}, f32[128,128]{1,0:T(8,128)}, u32[]{:S(2)}) copy-start(f32[128,128]{1,0:T(8,128)} %convolution_bitcast_fusion.28) | copy-start | bytes 196612
  298.2 26.6 %copy-start.137 = (f32[128,128]{1,0:T(8,128)S(1)}, f32[128,128]{1,0:T(8,128)}, u32[]{:S(2)}) copy-start(f32[128,128]{1,0:T(8,128)} %convolution_bitcast_fusion.36) | copy-start | bytes 196612
  298.2 26.6 %copy-start.139 = (f32[128,128]{1,0:T(8,128)S(1)}, f32[128,128]{1,0:T(8,128)}, u32[]{:S(2)}) copy-start(f32[128,128]{1,0:T(8,128)} %convolution_bitcast_fusion.27) | copy-start | bytes 196612
  318.3 8.9 %all-to-all-start.6 = ((bf16[4,2,15360]{2,1,0:T(2,128)(2,1)}), bf16[4,2,15360]{2,1,0:T(2,128)(2,1)S(1)}, u32[]{:S(2)}, u32[]{:S(2)}) async-start(bf16[4,2,15360]{2,1,0:T(2,128)(2,1)} %reshape.1689), calls=%async_computation.6 | async-start | bytes 491520 | tf_op jit(solution)/shard_map/all_to_all | solution.py:119
  353.1 4.5 collective-permute-start.8
  355.3 5.9 collective-permute-start.10
  356.8 4.3 collective-permute-start.9
  369.8 9.7 %all-to-all-start.2 = ((bf16[8,6,2560]{2,1,0:T(8,128)(2,1)}), bf16[8,6,2560]{2,1,0:T(8,128)(2,1)}, u32[]{:S(2)}, u32[]{:S(2)}) async-start(bf16[8,6,2560]{2,1,0:T(8,128)(2,1)} %reshape.1684), calls=%async_computation.2 | async-start | bytes 655360 | tf_op jit(solution)/shard_map/all_to_all | solution.py:123
  419.4 57.1 %collective-permute-start.11 = (bf16[2,6,10240]{2,0,1:T(2,128)(2,1)S(1)}, bf16[2,6,10240]{2,0,1:T(2,128)(2,1)S(1)}, u32[]{:S(2)}, u32[]{:S(2)}) collective-permute-start(bf16[2,6,10240]{2,0,1:T(2,128)(2,1)S(1)} %add_convert_fusion.2), channel_id=1, source_target_pairs={{8,0},{16,8},{24,16},{9,1},{17,9},{25,17},{10,2},{18,10},{26,18},{... | collective-permute-start | bytes 737288 | tf_op jit(solution)/shard_map/ppermute | solution.py:12
  421.8 24.0 %copy-start.162 = (f32[128,128]{1,0:T(8,128)S(1)}, f32[128,128]{1,0:T(8,128)}, u32[]{:S(2)}) copy-start(f32[128,128]{1,0:T(8,128)} %convolution_bitcast_fusion.25) | copy-start | bytes 196612
  421.8 24.7 %copy-start.161 = (f32[128,128]{1,0:T(8,128)S(1)}, f32[128,128]{1,0:T(8,128)}, u32[]{:S(2)}) copy-start(f32[128,128]{1,0:T(8,128)} %convolution_bitcast_fusion.24) | copy-start | bytes 196612
  421.8 25.4 %copy-start.159 = (f32[128,128]{1,0:T(8,128)S(1)}, f32[128,128]{1,0:T(8,128)}, u32[]{:S(2)}) copy-start(f32[128,128]{1,0:T(8,128)} %convolution_bitcast_fusion.23) | copy-start | bytes 196612
  421.8 26.1 %copy-start.156 = (f32[128,128]{1,0:T(8,128)S(1)}, f32[128,128]{1,0:T(8,128)}, u32[]{:S(2)}) copy-start(f32[128,128]{1,0:T(8,128)} %convolution_bitcast_fusion.22) | copy-start | bytes 196612
  421.8 26.8 %copy-start.152 = (f32[128,128]{1,0:T(8,128)S(1)}, f32[128,128]{1,0:T(8,128)}, u32[]{:S(2)}) copy-start(f32[128,128]{1,0:T(8,128)} %convolution_bitcast_fusion.21) | copy-start | bytes 196612
  421.8 27.5 %copy-start.148 = (f32[128,128]{1,0:T(8,128)S(1)}, f32[128,128]{1,0:T(8,128)}, u32[]{:S(2)}) copy-start(f32[128,128]{1,0:T(8,128)} %convolution_bitcast_fusion.20) | copy-start | bytes 196612
  421.8 28.2 %copy-start.144 = (f32[128,128]{1,0:T(8,128)S(1)}, f32[128,128]{1,0:T(8,128)}, u32[]{:S(2)}) copy-start(f32[128,128]{1,0:T(8,128)} %convolution_bitcast_fusion.19) | copy-start | bytes 196612
  442.0 9.1 %all-to-all-start.7 = ((bf16[4,2,15360]{2,1,0:T(2,128)(2,1)}), bf16[4,2,15360]{2,1,0:T(2,128)(2,1)S(1)}, u32[]{:S(2)}, u32[]{:S(2)}) async-start(bf16[4,2,15360]{2,1,0:T(2,128)(2,1)} %reshape.1691), calls=%async_computation.7 | async-start | bytes 491520 | tf_op jit(solution)/shard_map/all_to_all | solution.py:119
  477.0 4.5 collective-permute-start.12
  479.6 5.9 collective-permute-start.14
  481.1 4.3 collective-permute-start.13
  494.1 9.7 %all-to-all-start.3 = ((bf16[8,6,2560]{2,1,0:T(8,128)(2,1)}), bf16[8,6,2560]{2,1,0:T(8,128)(2,1)}, u32[]{:S(2)}, u32[]{:S(2)}) async-start(bf16[8,6,2560]{2,1,0:T(8,128)(2,1)} %reshape.1685), calls=%async_computation.3 | async-start | bytes 655360 | tf_op jit(solution)/shard_map/all_to_all | solution.py:123
  543.6 56.3 %collective-permute-start.15 = (bf16[2,6,10240]{2,0,1:T(2,128)(2,1)S(1)}, bf16[2,6,10240]{2,0,1:T(2,128)(2,1)S(1)}, u32[]{:S(2)}, u32[]{:S(2)}) collective-permute-start(bf16[2,6,10240]{2,0,1:T(2,128)(2,1)S(1)} %add_convert_fusion.1), channel_id=1, source_target_pairs={{8,0},{16,8},{24,16},{9,1},{17,9},{25,17},{10,2},{18,10},{26,18},{... | collective-permute-start | bytes 737288 | tf_op jit(solution)/shard_map/ppermute | solution.py:12
  545.5 23.8 %copy-start.118 = (f32[9,64,64]{2,1,0:T(8,128)S(1)}, f32[9,64,64]{2,1,0:T(8,128)}, u32[]{:S(2)}) copy-start(f32[9,64,64]{2,1,0:T(8,128)} %constant_dynamic-update-slice_fusion.35) | copy-start | bytes 442372
  545.6 26.3 %copy-start.157 = (f32[128,128]{1,0:T(8,128)S(1)}, f32[128,128]{1,0:T(8,128)}, u32[]{:S(2)}) copy-start(f32[128,128]{1,0:T(8,128)} %convolution_bitcast_fusion.13) | copy-start | bytes 196612
  545.6 26.4 %copy-start.153 = (f32[128,128]{1,0:T(8,128)S(1)}, f32[128,128]{1,0:T(8,128)}, u32[]{:S(2)}) copy-start(f32[128,128]{1,0:T(8,128)} %convolution_bitcast_fusion.12) | copy-start | bytes 196612
  545.6 26.5 %copy-start.149 = (f32[128,128]{1,0:T(8,128)S(1)}, f32[128,128]{1,0:T(8,128)}, u32[]{:S(2)}) copy-start(f32[128,128]{1,0:T(8,128)} %convolution_bitcast_fusion.11) | copy-start | bytes 196612
  545.6 26.5 %copy-start.145 = (f32[128,128]{1,0:T(8,128)S(1)}, f32[128,128]{1,0:T(8,128)}, u32[]{:S(2)}) copy-start(f32[128,128]{1,0:T(8,128)} %convolution_bitcast_fusion.10) | copy-start | bytes 196612
  545.6 26.6 %copy-start.138 = (f32[128,128]{1,0:T(8,128)S(1)}, f32[128,128]{1,0:T(8,128)}, u32[]{:S(2)}) copy-start(f32[128,128]{1,0:T(8,128)} %convolution_bitcast_fusion.18) | copy-start | bytes 196612
  545.6 26.6 %copy-start.140 = (f32[128,128]{1,0:T(8,128)S(1)}, f32[128,128]{1,0:T(8,128)}, u32[]{:S(2)}) copy-start(f32[128,128]{1,0:T(8,128)} %convolution_bitcast_fusion.9) | copy-start | bytes 196612
  565.7 8.9 %all-to-all-start.8 = ((bf16[4,2,15360]{2,1,0:T(2,128)(2,1)}), bf16[4,2,15360]{2,1,0:T(2,128)(2,1)S(1)}, u32[]{:S(2)}, u32[]{:S(2)}) async-start(bf16[4,2,15360]{2,1,0:T(2,128)(2,1)} %reshape.1693), calls=%async_computation.8 | async-start | bytes 491520 | tf_op jit(solution)/shard_map/all_to_all | solution.py:119
  600.5 4.5 collective-permute-start.16
  602.7 6.2 collective-permute-start.18
  604.2 4.6 collective-permute-start.17
  614.0 9.1 %all-to-all-start.4 = ((bf16[8,6,2560]{2,1,0:T(8,128)(2,1)}), bf16[8,6,2560]{2,1,0:T(8,128)(2,1)S(1)}, u32[]{:S(2)}, u32[]{:S(2)}) async-start(bf16[8,6,2560]{2,1,0:T(8,128)(2,1)} %reshape.1686), calls=%async_computation.4 | async-start | bytes 655360 | tf_op jit(solution)/shard_map/all_to_all | solution.py:123
  617.6 127.6 %all-reduce.17.cloned.1.call-start = ((), (), s32[]{:S(2)}) async-start(), calls=%async_computation.10 | async-start | bytes 589824 | tf_op jit(solution)/shard_map/psum | solution.py:157
  686.0 8.9 %all-to-all-start.9 = ((bf16[4,2,15360]{2,1,0:T(2,128)(2,1)}), bf16[4,2,15360]{2,1,0:T(2,128)(2,1)S(1)}, u32[]{:S(2)}, u32[]{:S(2)}) async-start(bf16[4,2,15360]{2,1,0:T(2,128)(2,1)} %reshape.1695), calls=%async_computation.9 | async-start | bytes 491520 | tf_op jit(solution)/shard_map/all_to_all | solution.py:119
  (130 other events, 1444.9 us)
Sparse Core Ops, SparseCore 0:
  645.2 53.1 all-reduce.16
